TPU v7x, 32 devices: a whole 2x2x4 slice. The times are simulated.
32 devices in a mesh: box: 32 (over z, y, x, core).
Axes of the slice: x: 2, y: 2, z: 4, core: 2. Of those that a mesh axis runs over, the one named last changes fastest.
Arguments:
- fine_mult: bfloat16 [32768, 128], P('box'), may hold values from -6 to 6
- parent_mult: bfloat16 [4096, 128], P('box'), may hold values from -6 to 6
- fine_mask: int32 [20, 32768], P(None, 'box'), may hold values from 0 to 65535, as said below
- parent_mask: int32 [20, 4096], P(None, 'box'), may hold values from 0 to 65535, as said below
- kernels: bfloat16 [316, 128, 128], replicated, may hold values from -0.0390625 to 0.0390625
- shift_ops: bfloat16 [8, 128, 128], replicated, may hold values from -0.5 to 0.5
Outputs:
- fine_local: bfloat16 [32768, 128], P('box')
- parent_local: bfloat16 [4096, 128], P('box')
Inputs may be any that keep to these rules, and one draw needn't show every extreme that they name: `fine_mask`: bit d mod 16 of word floor(d / 16) of box t is set only where the box at t's coordinates plus offset d lies inside the grid and its parent is one of the 27 boxes around t's parent; bits 12 to 15 of word 19 are zero; sources in many regions are missing from the lists. `parent_mask`: the same rule at the parent level.
All inputs are finite; a program needn't handle non-finite values.
Results may differ from a plain program's by a relative error of at most 0.0027.
Values may be sent and summed in bfloat16 or wider, within the bound.
A program may use at most 320 MiB of HBM per device.

v0:
```python
import functools

import jax
import jax.numpy as jnp
import numpy as np
from jax import lax
from jax.experimental import pallas as pl
from jax.experimental.pallas import tpu as pltpu
from jax.sharding import PartitionSpec as P

CHUNK = 9


def direction_table():
    listing = []
    for g1 in range(3):
        for g2 in range(3):
            for g3 in range(3):
                spans = [([-2, -1, 0, 1, 2], [-3], [3])[g] for g in (g1, g2, g3)]
                for o1 in spans[0]:
                    for o2 in spans[1]:
                        for o3 in spans[2]:
                            if max(abs(o1), abs(o2), abs(o3)) >= 2:
                                listing.append((o1, o2, o3))
    return listing


def class_tables():
    dirs, wins = [], []
    for c in range(8):
        child = (c >> 2 & 1, c >> 1 & 1, c & 1)
        count = 0
        for number, offset in enumerate(direction_table()):
            moved = [child[k] + offset[k] for k in range(3)]
            shift = [m >> 1 for m in moved]
            if max(abs(s) for s in shift) > 1:
                continue
            source = (moved[0] & 1) * 4 + (moved[1] & 1) * 2 + (moved[2] & 1)
            delta = (shift[0] + 1) * 9 + (shift[1] + 1) * 3 + shift[2] + 1
            dirs.append(number)
            wins.append(delta * 8 + source)
            count += 1
        assert count == 189
    return np.array(dirs, np.int32), np.array(wins, np.int32)


def grid_order(total_bits):
    order, extents = [], []
    for target in range(3):
        chosen = [k for k in range(total_bits - 1, -1, -1) if 2 - k % 3 == target]
        order += [total_bits - 1 - k for k in chosen]
        extents.append(2 ** len(chosen))
    return order, extents


def to_grid(rows, total_bits):
    order, extents = grid_order(total_bits)
    trailing = rows.shape[1:]
    bitwise = rows.reshape((2,) * total_bits + trailing)
    kept = tuple(range(total_bits, total_bits + len(trailing)))
    return jnp.transpose(bitwise, tuple(order) + kept).reshape(tuple(extents) + trailing)


def grid_index(morton, extents):
    coords = [0, 0, 0]
    for k in range(morton.bit_length()):
        coords[2 - k % 3] |= (morton >> k & 1) << (k // 3)
    return (coords[0] * extents[1] + coords[1]) * extents[2] + coords[2]


def shift_route(count, level_bits, dim, step):
    bits = count.bit_length() - 1
    owned = [k for k in range(bits) if 2 - (level_bits + k) % 3 == dim]
    route = []
    for src in range(count):
        at = sum((src >> k & 1) << n for n, k in enumerate(owned)) + step
        if 0 <= at < 2 ** len(owned):
            dst = src
            for n, k in enumerate(owned):
                dst = dst & ~(1 << k) | (at >> n & 1) << k
            route.append((src, dst))
    return route


def extend(blocks, level_bits, count):
    for dim in range(3):
        halos = []
        for step in (1, -1):
            faces = []
            for block in blocks:
                size = block.shape[dim]
                start = size - 1 if step == 1 else 0
                faces.append(lax.slice_in_dim(block, start, start + 1, axis=dim))
            flat = jnp.concatenate([f.reshape((-1,) + f.shape[3:]) for f in faces])
            got = lax.ppermute(flat, "box", shift_route(count, level_bits, dim, step))
            parts, row = [], 0
            for f in faces:
                rows = f.shape[0] * f.shape[1] * f.shape[2]
                parts.append(got[row : row + rows].reshape(f.shape))
                row += rows
            halos.append(parts)
        blocks = [
            jnp.concatenate([low, block, high], axis=dim)
            for low, block, high in zip(halos[0], blocks, halos[1])
        ]
    return blocks


def interact_kernel(
    fext, gext, dtab, wtab, ext_f, ext_p, words, bits, shift, kernels,
    fine_out, parent_out, kv, win, wb, acc_f, acc_p, par, sem,
):
    nf, ng = fext[0] * fext[1] * fext[2], gext[0] * gext[1] * gext[2]
    rows = nf + ng
    tiles = rows // 16
    fetch = pltpu.make_async_copy(kernels, kv, sem)
    fetch.start()

    def build(index, carry):
        delta, source = index // 8, index % 8
        dx, dy, dz = delta // 9, delta // 3 % 3, delta % 3
        for ref, ext, base in ((ext_f, fext, 0), (ext_p, gext, nf)):
            got = []
            for x in range(ext[0]):
                for y in range(ext[1]):
                    first = ((x + dx) * (ext[1] + 2) + y + dy) * (ext[2] + 2) + dz
                    got.append(ref[pl.ds(first * 8 + source, ext[2], stride=8), :])
            stack = jnp.concatenate(got, axis=0).astype(jnp.bfloat16)
            count = stack.shape[0] // 16
            win[index, pl.ds(base // 16, count)] = stack.reshape(count, 16, 128)
        return carry

    lax.fori_loop(0, 216, build, 0)
    fetch.wait()

    def one_class(c, carry):
        mine = words[c]
        for w in range(20):
            spread = jnp.broadcast_to(mine[:, w : w + 1], (rows, 128)).astype(jnp.int16)
            wb[w] = spread.reshape(tiles, 16, 128)

        def step(j, acc):
            lhs, rhs = [], []
            for i in range(CHUNK):
                n = c * 189 + j * CHUNK + i
                d = dtab[n]
                hit = (wb[d // 16] & bits[d % 16][None]) != 0
                x = win[wtab[n]]
                lhs.append(jnp.where(hit, x, jnp.zeros_like(x)).reshape(rows, 128))
                rhs.append(kv[d])
            return acc + jnp.dot(
                jnp.concatenate(lhs, axis=1),
                jnp.concatenate(rhs, axis=0),
                preferred_element_type=jnp.float32,
            )

        acc = lax.fori_loop(0, 189 // CHUNK, step, jnp.zeros((rows, 128), jnp.float32))
        acc_f[pl.ds(pl.multiple_of(c * nf, 16), nf), :] = acc[:nf]
        acc_p[pl.ds(pl.multiple_of(c * ng, 16), ng), :] = (
            (acc[nf:] * 0.5).astype(jnp.bfloat16).astype(jnp.float32)
        )
        return carry

    lax.fori_loop(0, 8, one_class, 0)

    for c in range(8):
        cx, cy, cz = c >> 2 & 1, c >> 1 & 1, c & 1
        for gx in range(gext[0]):
            for gy in range(gext[1]):
                first = c * ng + (gx * gext[1] + gy) * gext[2]
                to = ((2 * gx + cx) * fext[1] + 2 * gy + cy) * fext[2] + cz
                par[pl.ds(to, gext[2], stride=2), :] = acc_p[pl.ds(first, gext[2]), :]
    local = par[...].astype(jnp.bfloat16)
    for c in range(8):
        acc_f[pl.ds(c * nf, nf), :] += jnp.dot(
            local, shift[c], preferred_element_type=jnp.float32
        )
    for ref, out, ext, total in ((acc_f, fine_out, fext, nf), (acc_p, parent_out, gext, ng)):
        for m in range(0, total, 2):
            pair = [
                ref[pl.ds(grid_index(m + k, ext), 8, stride=total), :] for k in range(2)
            ]
            out[pl.ds(m * 8, 16), :] = jnp.concatenate(pair, axis=0).astype(jnp.bfloat16)


def on_device(fine_mult, parent_mult, fine_mask, parent_mask, kernels, shift_ops):
    count = lax.axis_size("box")
    width = fine_mult.shape[1]
    fbits = fine_mult.shape[0].bit_length() - 4
    pbits = parent_mult.shape[0].bit_length() - 4
    fext, gext = tuple(grid_order(fbits)[1]), tuple(grid_order(pbits)[1])
    nf, ng = 2**fbits, 2**pbits
    rows = nf + ng

    blocks = [
        to_grid(fine_mult.reshape(nf, 8, width), fbits),
        to_grid(parent_mult.reshape(ng, 8, width), pbits),
    ]
    ext_f, ext_p = (
        b.reshape(-1, width).astype(jnp.float32) for b in extend(blocks, fbits + 3, count)
    )

    def by_class(mask, bits, total):
        grid = to_grid(jnp.transpose(mask).reshape(total, 8, 20), bits)
        return jnp.transpose(grid.reshape(total, 8, 20), (1, 0, 2))

    words = jnp.concatenate(
        [by_class(fine_mask, fbits, nf), by_class(parent_mask, pbits, ng)], axis=1
    )
    dtab, wtab = class_tables()
    flags = np.array([1 << k if k < 15 else -(1 << 15) for k in range(16)], np.int16)
    bits = np.broadcast_to(flags[:, None, None], (16, 16, 128))
    smem = pl.BlockSpec(memory_space=pltpu.SMEM)
    vmem = pl.BlockSpec(memory_space=pltpu.VMEM)
    return pl.pallas_call(
        functools.partial(interact_kernel, fext, gext),
        out_shape=[
            jax.ShapeDtypeStruct(fine_mult.shape, jnp.bfloat16),
            jax.ShapeDtypeStruct(parent_mult.shape, jnp.bfloat16),
        ],
        in_specs=[smem, smem, vmem, vmem, vmem, vmem, vmem, pl.BlockSpec(memory_space=pl.ANY)],
        out_specs=[vmem, vmem],
        scratch_shapes=[
            pltpu.VMEM(kernels.shape, jnp.bfloat16),
            pltpu.VMEM((216, rows // 16, 16, width), jnp.bfloat16),
            pltpu.VMEM((20, rows // 16, 16, width), jnp.int16),
            pltpu.VMEM((8 * nf, width), jnp.float32),
            pltpu.VMEM((8 * ng, width), jnp.float32),
            pltpu.VMEM((nf, width), jnp.float32),
            pltpu.SemaphoreType.DMA,
        ],
        compiler_params=pltpu.CompilerParams(vmem_limit_bytes=56 * 1024 * 1024),
        cost_estimate=pl.CostEstimate(
            flops=2 * 8 * rows * 189 * width * width,
            bytes_accessed=kernels.size * 2,
            transcendentals=0,
        ),
        name="interact",
    )(dtab, wtab, ext_f, ext_p, words, jnp.asarray(bits), shift_ops, kernels)


def solution(mesh):
    return jax.shard_map(
        on_device,
        mesh=mesh,
        in_specs=(P("box", None), P("box", None), P(None, "box"), P(None, "box"), P(), P()),
        out_specs=(P("box", None), P("box", None)),
        check_vma=False,
    )
```

profile of v0, /device:TPU:3, one launch (start us, length us, event | category | flops | bytes accessed | tf_op | source)
XLA Modules:
  0.0 103.3 jit_solution(17720641188344127272)
XLA Ops:
  0.6 0.0 copy-start
  0.6 1.0 copy.53
  1.7 0.7 fusion.2
  2.4 4.2 %collective-permute-start = (bf16[40,8,128]{2,1,0:T(8,128)(2,1)S(1)}, bf16[40,8,128]{2,1,0:T(8,128)(2,1)S(1)}, u32[]{:S(2)}, u32[]{:S(2)}) collective-permute-start(bf16[40,8,128]{2,1,0:T(8,128)(2,1)S(1)} %pad_maximum_fusion.9), channel_id=1, source_target_pairs={{0,2},{1,3},{2,16},{3,17},{4,6},{5,7},{6,20},{7,21},{8,10},{9,11},... | collective-permute-start | bytes 245768 | tf_op jit(solution)/shard_map/ppermute | solution.py:95
  6.7 1.9 %collective-permute-start.1 = (bf16[40,8,128]{2,1,0:T(8,128)(2,1)S(1)}, bf16[40,8,128]{2,1,0:T(8,128)(2,1)S(1)}, u32[]{:S(2)}, u32[]{:S(2)}) collective-permute-start(bf16[40,8,128]{2,1,0:T(8,128)(2,1)S(1)} %pad_maximum_fusion.10), channel_id=1, source_target_pairs={{2,0},{3,1},{6,4},{7,5},{10,8},{11,9},{14,12},{15,13},{16,2},{17,3... | collective-permute-start | bytes 245768 | tf_op jit(solution)/shard_map/ppermute | solution.py:95
  8.6 0.8 copy.56
  9.4 0.0 collective-permute-done
  9.4 4.3 %collective-permute-done.1 = bf16[40,8,128]{2,1,0:T(8,128)(2,1)S(1)} collective-permute-done((bf16[40,8,128]{2,1,0:T(8,128)(2,1)S(1)}, bf16[40,8,128]{2,1,0:T(8,128)(2,1)S(1)}, u32[]{:S(2)}, u32[]{:S(2)}) %collective-permute-start.1) | collective-permute-done | bytes 81952 | tf_op jit(solution)/shard_map/ppermute | solution.py:95
  13.8 5.3 %collective-permute-start.2 = (bf16[64,8,128]{2,1,0:T(8,128)(2,1)S(1)}, bf16[64,8,128]{2,1,0:T(8,128)(2,1)S(1)}, u32[]{:S(2)}, u32[]{:S(2)}) collective-permute-start(bf16[64,8,128]{2,1,0:T(8,128)(2,1)S(1)} %pad_maximum_fusion.2), channel_id=1, source_target_pairs={{0,1},{1,8},{2,3},{3,10},{4,5},{5,12},{6,7},{7,14},{8,9},{10,11},{... | collective-permute-start | bytes 393224 | tf_op jit(solution)/shard_map/ppermute | solution.py:95
  19.1 0.0 copy-start.1
  19.1 1.9 %collective-permute-start.3 = (bf16[64,8,128]{2,1,0:T(8,128)(2,1)S(1)}, bf16[64,8,128]{2,1,0:T(8,128)(2,1)S(1)}, u32[]{:S(2)}, u32[]{:S(2)}) collective-permute-start(bf16[64,8,128]{2,1,0:T(8,128)(2,1)S(1)} %pad_maximum_fusion.3), channel_id=1, source_target_pairs={{1,0},{3,2},{5,4},{7,6},{8,1},{9,8},{10,3},{11,10},{12,5},{13,12},... | collective-permute-start | bytes 393224 | tf_op jit(solution)/shard_map/ppermute | solution.py:95
  21.0 0.0 copy-done
  21.0 0.2 copy.57
  21.3 0.1 copy.58
  21.3 0.1 copy.65
  21.4 0.0 copy-done.1
  21.4 0.1 copy.60
  21.6 0.0 collective-permute-done.2
  21.6 3.8 %collective-permute-done.3 = bf16[64,8,128]{2,1,0:T(8,128)(2,1)S(1)} collective-permute-done((bf16[64,8,128]{2,1,0:T(8,128)(2,1)S(1)}, bf16[64,8,128]{2,1,0:T(8,128)(2,1)S(1)}, u32[]{:S(2)}, u32[]{:S(2)}) %collective-permute-start.3) | collective-permute-done | bytes 131104 | tf_op jit(solution)/shard_map/ppermute | solution.py:95
  25.5 3.1 %collective-permute-start.4 = (bf16[52,8,128]{2,1,0:T(8,128)(2,1)S(1)}, bf16[52,8,128]{2,1,0:T(8,128)(2,1)S(1)}, u32[]{:S(2)}, u32[]{:S(2)}) collective-permute-start(bf16[52,8,128]{2,1,0:T(8,128)(2,1)S(1)} %pad_maximum_fusion.4), channel_id=1, source_target_pairs={{0,4},{1,5},{2,6},{3,7},{8,12},{9,13},{10,14},{11,15},{16,20},{17,... | collective-permute-start | bytes 319496 | tf_op jit(solution)/shard_map/ppermute | solution.py:95
  28.7 1.3 %collective-permute-start.5 = (bf16[52,8,128]{2,1,0:T(8,128)(2,1)S(1)}, bf16[52,8,128]{2,1,0:T(8,128)(2,1)S(1)}, u32[]{:S(2)}, u32[]{:S(2)}) collective-permute-start(bf16[52,8,128]{2,1,0:T(8,128)(2,1)S(1)} %pad_maximum_fusion.5), channel_id=1, source_target_pairs={{4,0},{5,1},{6,2},{7,3},{12,8},{13,9},{14,10},{15,11},{20,16},{21,... | collective-permute-start | bytes 319496 | tf_op jit(solution)/shard_map/ppermute | solution.py:95
  30.0 0.9 pad_add_fusion.words
  30.9 0.0 collective-permute-done.4
  30.9 3.3 %collective-permute-done.5 = bf16[52,8,128]{2,1,0:T(8,128)(2,1)S(1)} collective-permute-done((bf16[52,8,128]{2,1,0:T(8,128)(2,1)S(1)}, bf16[52,8,128]{2,1,0:T(8,128)(2,1)S(1)}, u32[]{:S(2)}, u32[]{:S(2)}) %collective-permute-start.5) | collective-permute-done | bytes 106528 | tf_op jit(solution)/shard_map/ppermute | solution.py:95
  34.1 0.1 pad_maximum_fusion.1
  34.2 0.8 bitcast_convert_fusion.1.ext_p
  35.0 0.0 copy-start.2
  35.0 0.2 pad_maximum_fusion
  35.2 1.3 %bitcast_convert_fusion.ext_f = f32[2880,128]{1,0:T(8,128)} fusion(bf16[6,6,10,8,128]{4,3,2,1,0:T(8,128)(2,1)S(1)} %pad_maximum_fusion), kind=kLoop, calls=%fused_computation.1 | loop fusion | flops 368640 | bytes 2211840 | tf_op jit(solution)/shard_map/convert_element_type | solution.py:200
  36.5 0.0 copy-done.2
  36.5 0.7 jit_solution_.3.bits
  37.2 66.1 %interact.1 = (bf16[1024,128]{1,0:T(8,128)(2,1)}, bf16[128,128]{1,0:T(8,128)(2,1)}) custom-call(s32[1512]{0:T(1024)} %constant.7.clone.dtab, s32[1512]{0:T(1024)} %constant.8.clone.wtab, f32[2880,128]{1,0:T(8,128)} %bitcast_convert_fusion.ext_f, f32[768,128]{1,0:T(8,128)} %bitcast_convert_fusion.1.ext_p, s32[8,144,20]{2,1,0:T(8,128)} %pad_add_fusion.words, ...), custom_call_target="tpu_custom_call" | custom-call | flops 7134511104 | bytes 10354688 | tf_op jit(solution)/shard_map/interact/pallas_call | solution.py:215
  (28 shorter events, 0.3 us)
Async XLA Ops:
  0.6 20.4 %copy-start = (s32[20,1024]{1,0:T(8,128)S(1)}, s32[20,1024]{1,0:T(8,128)}, u32[]{:S(2)}) copy-start(s32[20,1024]{1,0:T(8,128)} %param.11) | copy-start | bytes 245764
  2.4 6.9 %collective-permute-start = (bf16[40,8,128]{2,1,0:T(8,128)(2,1)S(1)}, bf16[40,8,128]{2,1,0:T(8,128)(2,1)S(1)}, u32[]{:S(2)}, u32[]{:S(2)}) collective-permute-start(bf16[40,8,128]{2,1,0:T(8,128)(2,1)S(1)} %pad_maximum_fusion.9), channel_id=1, source_target_pairs={{0,2},{1,3},{2,16},{3,17},{4,6},{5,7},{6,20},{7,21},{8,10},{9,11},... | collective-permute-start | bytes 245768 | tf_op jit(solution)/shard_map/ppermute | solution.py:95
  6.7 7.0 %collective-permute-start.1 = (bf16[40,8,128]{2,1,0:T(8,128)(2,1)S(1)}, bf16[40,8,128]{2,1,0:T(8,128)(2,1)S(1)}, u32[]{:S(2)}, u32[]{:S(2)}) collective-permute-start(bf16[40,8,128]{2,1,0:T(8,128)(2,1)S(1)} %pad_maximum_fusion.10), channel_id=1, source_target_pairs={{2,0},{3,1},{6,4},{7,5},{10,8},{11,9},{14,12},{15,13},{16,2},{17,3... | collective-permute-start | bytes 245768 | tf_op jit(solution)/shard_map/ppermute | solution.py:95
  13.8 7.8 %collective-permute-start.2 = (bf16[64,8,128]{2,1,0:T(8,128)(2,1)S(1)}, bf16[64,8,128]{2,1,0:T(8,128)(2,1)S(1)}, u32[]{:S(2)}, u32[]{:S(2)}) collective-permute-start(bf16[64,8,128]{2,1,0:T(8,128)(2,1)S(1)} %pad_maximum_fusion.2), channel_id=1, source_target_pairs={{0,1},{1,8},{2,3},{3,10},{4,5},{5,12},{6,7},{7,14},{8,9},{10,11},{... | collective-permute-start | bytes 393224 | tf_op jit(solution)/shard_map/ppermute | solution.py:95
  19.1 2.4 %copy-start.1 = (s32[20,128]{1,0:T(8,128)S(1)}, s32[20,128]{1,0:T(8,128)}, u32[]{:S(2)}) copy-start(s32[20,128]{1,0:T(8,128)} %param.12) | copy-start | bytes 30724
  19.1 6.3 %collective-permute-start.3 = (bf16[64,8,128]{2,1,0:T(8,128)(2,1)S(1)}, bf16[64,8,128]{2,1,0:T(8,128)(2,1)S(1)}, u32[]{:S(2)}, u32[]{:S(2)}) collective-permute-start(bf16[64,8,128]{2,1,0:T(8,128)(2,1)S(1)} %pad_maximum_fusion.3), channel_id=1, source_target_pairs={{1,0},{3,2},{5,4},{7,6},{8,1},{9,8},{10,3},{11,10},{12,5},{13,12},... | collective-permute-start | bytes 393224 | tf_op jit(solution)/shard_map/ppermute | solution.py:95
  25.5 5.4 %collective-permute-start.4 = (bf16[52,8,128]{2,1,0:T(8,128)(2,1)S(1)}, bf16[52,8,128]{2,1,0:T(8,128)(2,1)S(1)}, u32[]{:S(2)}, u32[]{:S(2)}) collective-permute-start(bf16[52,8,128]{2,1,0:T(8,128)(2,1)S(1)} %pad_maximum_fusion.4), channel_id=1, source_target_pairs={{0,4},{1,5},{2,6},{3,7},{8,12},{9,13},{10,14},{11,15},{16,20},{17,... | collective-permute-start | bytes 319496 | tf_op jit(solution)/shard_map/ppermute | solution.py:95
  28.7 5.4 %collective-permute-start.5 = (bf16[52,8,128]{2,1,0:T(8,128)(2,1)S(1)}, bf16[52,8,128]{2,1,0:T(8,128)(2,1)S(1)}, u32[]{:S(2)}, u32[]{:S(2)}) collective-permute-start(bf16[52,8,128]{2,1,0:T(8,128)(2,1)S(1)} %pad_maximum_fusion.5), channel_id=1, source_target_pairs={{4,0},{5,1},{6,2},{7,3},{12,8},{13,9},{14,10},{15,11},{20,16},{21,... | collective-permute-start | bytes 319496 | tf_op jit(solution)/shard_map/ppermute | solution.py:95
  35.0 1.5 %copy-start.2 = (s16[16]{0:T(256)(128)(2,1)S(1)}, s16[16]{0:T(256)(128)(2,1)}, u32[]{:S(2)}) copy-start(s16[16]{0:T(256)(128)(2,1)} %constant.6.clone) | copy-start | bytes 100
where the time goes:
time: 104 us; the launch traced here: 103 us
  Pallas kernels  66.1 us (64%)
  starting transfers between devices  17.8 us (17%)
  waiting for transfers between devices  11.3 us (11%)
  local copies, waits for them, and re-layouts  3.82 us (4%)
  other arithmetic  3.31 us (3%)
    pallas_call x1, Pallas kernels, on_device(): pl.pallas_call(functools.partial(interact_kernel, fext, gext), out_shape=...  66.1 us
    ppermute x6, starting transfers between devices, extend(): got = lax.ppermute(flat, 'box', shift_route(count, level_bits, dim, step))  17.8 us
    ppermute x6, waiting for transfers between devices, extend(): got = lax.ppermute(flat, 'box', shift_route(count, level_bits, dim, step))  11.3 us
  transfers between devices with their start and end apart: 6, of which 3 were waited for; matrix products, arithmetic and copies ran while one was open for 2% of the time, Pallas kernels for 0%

commit v1 on v0

--- a/solution.py
+++ b/solution.py
@@ -8,7 +8,7 @@
 from jax.experimental.pallas import tpu as pltpu
 from jax.sharding import PartitionSpec as P
 
-CHUNK = 9
+CHUNK = 14
 
 
 def direction_table():
@@ -25,23 +25,34 @@
     return listing
 
 
-def class_tables():
-    dirs, wins = [], []
+def window_table():
+    table = np.zeros((8, 316), np.int32)
     for c in range(8):
         child = (c >> 2 & 1, c >> 1 & 1, c & 1)
-        count = 0
         for number, offset in enumerate(direction_table()):
             moved = [child[k] + offset[k] for k in range(3)]
             shift = [m >> 1 for m in moved]
-            if max(abs(s) for s in shift) > 1:
-                continue
-            source = (moved[0] & 1) * 4 + (moved[1] & 1) * 2 + (moved[2] & 1)
-            delta = (shift[0] + 1) * 9 + (shift[1] + 1) * 3 + shift[2] + 1
-            dirs.append(number)
-            wins.append(delta * 8 + source)
-            count += 1
-        assert count == 189
-    return np.array(dirs, np.int32), np.array(wins, np.int32)
+            if max(abs(s) for s in shift) <= 1:
+                source = (moved[0] & 1) * 4 + (moved[1] & 1) * 2 + (moved[2] & 1)
+                delta = (shift[0] + 1) * 9 + (shift[1] + 1) * 3 + shift[2] + 1
+                table[c, number] = delta * 8 + source
+    return table.reshape(-1)
+
+
+def groups():
+    runs = []
+    for number, offset in enumerate(direction_table()):
+        classes = tuple(
+            c for c in range(8)
+            if all(
+                abs(offset[k]) < 3 or (c >> (2 - k) & 1) == (offset[k] < 0) for k in range(3)
+            )
+        )
+        if runs and runs[-1][2] == classes:
+            runs[-1][1] += 1
+        else:
+            runs.append([number, 1, classes])
+    return runs
 
 
 def grid_order(total_bits):
@@ -107,8 +118,8 @@
 
 
 def interact_kernel(
-    fext, gext, dtab, wtab, ext_f, ext_p, words, bits, shift, kernels,
-    fine_out, parent_out, kv, win, wb, acc_f, acc_p, par, sem,
+    fext, gext, wtab, ext_f, ext_p, words, bits, shift, kernels,
+    fine_out, parent_out, kv, win, wb, acc, acc_f, acc_p, par, sem,
 ):
     nf, ng = fext[0] * fext[1] * fext[2], gext[0] * gext[1] * gext[2]
     rows = nf + ng
@@ -133,36 +144,49 @@
     lax.fori_loop(0, 216, build, 0)
     fetch.wait()
 
-    def one_class(c, carry):
+    def spread(c, carry):
         mine = words[c]
         for w in range(20):
-            spread = jnp.broadcast_to(mine[:, w : w + 1], (rows, 128)).astype(jnp.int16)
-            wb[w] = spread.reshape(tiles, 16, 128)
-
-        def step(j, acc):
-            lhs, rhs = [], []
-            for i in range(CHUNK):
-                n = c * 189 + j * CHUNK + i
-                d = dtab[n]
-                hit = (wb[d // 16] & bits[d % 16][None]) != 0
-                x = win[wtab[n]]
-                lhs.append(jnp.where(hit, x, jnp.zeros_like(x)).reshape(rows, 128))
-                rhs.append(kv[d])
-            return acc + jnp.dot(
-                jnp.concatenate(lhs, axis=1),
-                jnp.concatenate(rhs, axis=0),
-                preferred_element_type=jnp.float32,
-            )
-
-        acc = lax.fori_loop(0, 189 // CHUNK, step, jnp.zeros((rows, 128), jnp.float32))
-        acc_f[pl.ds(pl.multiple_of(c * nf, 16), nf), :] = acc[:nf]
-        acc_p[pl.ds(pl.multiple_of(c * ng, 16), ng), :] = (
-            (acc[nf:] * 0.5).astype(jnp.bfloat16).astype(jnp.float32)
-        )
+            wide = jnp.broadcast_to(mine[:, w : w + 1], (rows, 128)).astype(jnp.int16)
+            wb[c, w] = wide.reshape(tiles, 16, 128)
+        acc[c] = jnp.zeros((rows, 128), jnp.float32)
         return carry
 
-    lax.fori_loop(0, 8, one_class, 0)
-
+    lax.fori_loop(0, 8, spread, 0)
+
+    def contract(start, count, classes):
+        lhs = []
+        for c in classes:
+            line = []
+            for i in range(count):
+                d = start + i
+                hit = (wb[c, d // 16] & bits[d % 16][None]) != 0
+                x = win[wtab[c * 316 + d]]
+                line.append(jnp.where(hit, x, jnp.zeros_like(x)).reshape(rows, 128))
+            lhs.append(jnp.concatenate(line, axis=1))
+        total = jnp.dot(
+            jnp.concatenate(lhs, axis=0),
+            kv[pl.ds(start, count)].reshape(count * 128, 128),
+            preferred_element_type=jnp.float32,
+        )
+        for k, c in enumerate(classes):
+            acc[c] += total[k * rows : (k + 1) * rows]
+
+    for start, count, classes in groups():
+        if count > CHUNK and len(classes) == 8:
+            def step(j, carry, start=start, classes=classes):
+                contract(start + j * CHUNK, CHUNK, classes)
+                return carry
+
+            lax.fori_loop(0, count // CHUNK, step, 0)
+        else:
+            contract(start, count, classes)
+
+    for c in range(8):
+        acc_f[pl.ds(c * nf, nf), :] = acc[c, :nf]
+        acc_p[pl.ds(c * ng, ng), :] = (
+            (acc[c, nf:] * 0.5).astype(jnp.bfloat16).astype(jnp.float32)
+        )
     for c in range(8):
         cx, cy, cz = c >> 2 & 1, c >> 1 & 1, c & 1
         for gx in range(gext[0]):
@@ -207,7 +231,7 @@
     words = jnp.concatenate(
         [by_class(fine_mask, fbits, nf), by_class(parent_mask, pbits, ng)], axis=1
     )
-    dtab, wtab = class_tables()
+    wtab = window_table()
     flags = np.array([1 << k if k < 15 else -(1 << 15) for k in range(16)], np.int16)
     bits = np.broadcast_to(flags[:, None, None], (16, 16, 128))
     smem = pl.BlockSpec(memory_space=pltpu.SMEM)
@@ -218,12 +242,13 @@
             jax.ShapeDtypeStruct(fine_mult.shape, jnp.bfloat16),
             jax.ShapeDtypeStruct(parent_mult.shape, jnp.bfloat16),
         ],
-        in_specs=[smem, smem, vmem, vmem, vmem, vmem, vmem, pl.BlockSpec(memory_space=pl.ANY)],
+        in_specs=[smem, vmem, vmem, vmem, vmem, vmem, pl.BlockSpec(memory_space=pl.ANY)],
         out_specs=[vmem, vmem],
         scratch_shapes=[
             pltpu.VMEM(kernels.shape, jnp.bfloat16),
             pltpu.VMEM((216, rows // 16, 16, width), jnp.bfloat16),
-            pltpu.VMEM((20, rows // 16, 16, width), jnp.int16),
+            pltpu.VMEM((8, 20, rows // 16, 16, width), jnp.int16),
+            pltpu.VMEM((8, rows, width), jnp.float32),
             pltpu.VMEM((8 * nf, width), jnp.float32),
             pltpu.VMEM((8 * ng, width), jnp.float32),
             pltpu.VMEM((nf, width), jnp.float32),
@@ -236,7 +261,7 @@
             transcendentals=0,
         ),
         name="interact",
-    )(dtab, wtab, ext_f, ext_p, words, jnp.asarray(bits), shift_ops, kernels)
+    )(wtab, ext_f, ext_p, words, jnp.asarray(bits), shift_ops, kernels)
 
 
 def solution(mesh):

time: 104 us -> 75.1 us (0.72)
  Pallas kernels: 66.1 us -> 37.5 us
    pallas_call x1, Pallas kernels: 66.1 us -> 37.5 us  [on_device(): pl.pallas_call(functools.partial(interact_kernel, fext, gext), out_shape=...]
  transfers between devices with their start and end apart: 6 -> 6, of which waited for: 3 -> 3; matrix products, arithmetic and copies ran while one was open for 2% -> 3% of each run, Pallas kernels for 0% -> 0%
where the time goes in v1:
time: 75.1 us; the launch traced here: 74.7 us
  Pallas kernels  37.5 us (50%)
  starting transfers between devices  17.8 us (24%)
  waiting for transfers between devices  11.3 us (15%)
  local copies, waits for them, and re-layouts  3.82 us (5%)
  other arithmetic  3.31 us (4%)
  between operations  0.92 us (1%)
    pallas_call x1, Pallas kernels, on_device(): pl.pallas_call(functools.partial(interact_kernel, fext, gext), out_shape=...  37.5 us
    ppermute x6, starting transfers between devices, extend(): got = lax.ppermute(flat, 'box', shift_route(count, level_bits, dim, step))  17.8 us
    ppermute x6, waiting for transfers between devices, extend(): got = lax.ppermute(flat, 'box', shift_route(count, level_bits, dim, step))  11.3 us
    convert_element_type x2, other arithmetic, on_device(): b.reshape(-1, width).astype(jnp.float32)  2.04 us
    transpose x4, local copies, waits for them, and re-layouts, to_grid(): jnp.transpose(bitwise, tuple(order) + kept)  1.83 us
  transfers between devices with their start and end apart: 6, of which 3 were waited for; matrix products, arithmetic and copies ran while one was open for 3% of the time, Pallas kernels for 0%

profile of v1, /device:TPU:3, one launch (start us, length us, event | category | flops | bytes accessed | tf_op | source)
XLA Modules:
  0.0 74.7 jit_solution(1988136223105078998)
XLA Ops:
  0.6 0.0 copy-start
  0.6 1.0 %copy.52 = bf16[2,2,2,2,2,2,2,8,128]{8,7,6,5,4,3,2,1,0:T(8,128)(2,1)S(1)} copy(bf16[2,2,2,2,2,2,2,8,128]{8,7,6,3,1,5,2,0,4:T(8,128)(2,1)} %bitcast.87) | data formatting | bytes 524288 | tf_op jit(solution)/shard_map/transpose | solution.py:72
  1.7 0.7 fusion.2
  2.4 4.2 %collective-permute-start = (bf16[40,8,128]{2,1,0:T(8,128)(2,1)S(1)}, bf16[40,8,128]{2,1,0:T(8,128)(2,1)S(1)}, u32[]{:S(2)}, u32[]{:S(2)}) collective-permute-start(bf16[40,8,128]{2,1,0:T(8,128)(2,1)S(1)} %pad_maximum_fusion.9), channel_id=1, source_target_pairs={{0,2},{1,3},{2,16},{3,17},{4,6},{5,7},{6,20},{7,21},{8,10},{9,11},... | collective-permute-start | bytes 245768 | tf_op jit(solution)/shard_map/ppermute | solution.py:106
  6.7 1.9 %collective-permute-start.1 = (bf16[40,8,128]{2,1,0:T(8,128)(2,1)S(1)}, bf16[40,8,128]{2,1,0:T(8,128)(2,1)S(1)}, u32[]{:S(2)}, u32[]{:S(2)}) collective-permute-start(bf16[40,8,128]{2,1,0:T(8,128)(2,1)S(1)} %pad_maximum_fusion.10), channel_id=1, source_target_pairs={{2,0},{3,1},{6,4},{7,5},{10,8},{11,9},{14,12},{15,13},{16,2},{17,3... | collective-permute-start | bytes 245768 | tf_op jit(solution)/shard_map/ppermute | solution.py:106
  8.6 0.8 %copy.55 = bf16[2,2,2,2,8,128]{5,4,3,2,1,0:T(8,128)(2,1)S(1)} copy(bf16[2,2,2,2,8,128]{5,4,3,1,0,2:T(8,128)(2,1)} %bitcast.101) | data formatting | bytes 65536 | tf_op jit(solution)/shard_map/transpose | solution.py:72
  9.4 0.0 collective-permute-done
  9.4 4.3 %collective-permute-done.1 = bf16[40,8,128]{2,1,0:T(8,128)(2,1)S(1)} collective-permute-done((bf16[40,8,128]{2,1,0:T(8,128)(2,1)S(1)}, bf16[40,8,128]{2,1,0:T(8,128)(2,1)S(1)}, u32[]{:S(2)}, u32[]{:S(2)}) %collective-permute-start.1) | collective-permute-done | bytes 81952 | tf_op jit(solution)/shard_map/ppermute | solution.py:106
  13.8 5.3 %collective-permute-start.2 = (bf16[64,8,128]{2,1,0:T(8,128)(2,1)S(1)}, bf16[64,8,128]{2,1,0:T(8,128)(2,1)S(1)}, u32[]{:S(2)}, u32[]{:S(2)}) collective-permute-start(bf16[64,8,128]{2,1,0:T(8,128)(2,1)S(1)} %pad_maximum_fusion.2), channel_id=1, source_target_pairs={{0,1},{1,8},{2,3},{3,10},{4,5},{5,12},{6,7},{7,14},{8,9},{10,11},{... | collective-permute-start | bytes 393224 | tf_op jit(solution)/shard_map/ppermute | solution.py:106
  19.1 0.0 copy-start.1
  19.1 1.9 %collective-permute-start.3 = (bf16[64,8,128]{2,1,0:T(8,128)(2,1)S(1)}, bf16[64,8,128]{2,1,0:T(8,128)(2,1)S(1)}, u32[]{:S(2)}, u32[]{:S(2)}) collective-permute-start(bf16[64,8,128]{2,1,0:T(8,128)(2,1)S(1)} %pad_maximum_fusion.3), channel_id=1, source_target_pairs={{1,0},{3,2},{5,4},{7,6},{8,1},{9,8},{10,3},{11,10},{12,5},{13,12},... | collective-permute-start | bytes 393224 | tf_op jit(solution)/shard_map/ppermute | solution.py:106
  21.0 0.0 copy-done
  21.0 0.2 copy.56
  21.3 0.1 copy.57
  21.3 0.1 copy.64
  21.4 0.0 copy-done.1
  21.4 0.1 copy.59
  21.6 0.0 collective-permute-done.2
  21.6 3.8 %collective-permute-done.3 = bf16[64,8,128]{2,1,0:T(8,128)(2,1)S(1)} collective-permute-done((bf16[64,8,128]{2,1,0:T(8,128)(2,1)S(1)}, bf16[64,8,128]{2,1,0:T(8,128)(2,1)S(1)}, u32[]{:S(2)}, u32[]{:S(2)}) %collective-permute-start.3) | collective-permute-done | bytes 131104 | tf_op jit(solution)/shard_map/ppermute | solution.py:106
  25.5 3.1 %collective-permute-start.4 = (bf16[52,8,128]{2,1,0:T(8,128)(2,1)S(1)}, bf16[52,8,128]{2,1,0:T(8,128)(2,1)S(1)}, u32[]{:S(2)}, u32[]{:S(2)}) collective-permute-start(bf16[52,8,128]{2,1,0:T(8,128)(2,1)S(1)} %pad_maximum_fusion.4), channel_id=1, source_target_pairs={{0,4},{1,5},{2,6},{3,7},{8,12},{9,13},{10,14},{11,15},{16,20},{17,... | collective-permute-start | bytes 319496 | tf_op jit(solution)/shard_map/ppermute | solution.py:106
  28.7 1.3 %collective-permute-start.5 = (bf16[52,8,128]{2,1,0:T(8,128)(2,1)S(1)}, bf16[52,8,128]{2,1,0:T(8,128)(2,1)S(1)}, u32[]{:S(2)}, u32[]{:S(2)}) collective-permute-start(bf16[52,8,128]{2,1,0:T(8,128)(2,1)S(1)} %pad_maximum_fusion.5), channel_id=1, source_target_pairs={{4,0},{5,1},{6,2},{7,3},{12,8},{13,9},{14,10},{15,11},{20,16},{21,... | collective-permute-start | bytes 319496 | tf_op jit(solution)/shard_map/ppermute | solution.py:106
  30.0 0.9 %pad_add_fusion.words = s32[8,144,20]{2,1,0:T(8,128)} fusion(s32[8,16,20]{2,1,0:T(8,128)S(1)} %bitcast.86, s32[8,128,20]{2,1,0:T(8,128)S(1)} %bitcast.60), kind=kLoop, calls=%fused_computation.2 | loop fusion | flops 23040 | bytes 184320 | tf_op jit(solution)/shard_map/concatenate | solution.py:231
  30.9 0.0 collective-permute-done.4
  30.9 3.3 %collective-permute-done.5 = bf16[52,8,128]{2,1,0:T(8,128)(2,1)S(1)} collective-permute-done((bf16[52,8,128]{2,1,0:T(8,128)(2,1)S(1)}, bf16[52,8,128]{2,1,0:T(8,128)(2,1)S(1)}, u32[]{:S(2)}, u32[]{:S(2)}) %collective-permute-start.5) | collective-permute-done | bytes 106528 | tf_op jit(solution)/shard_map/ppermute | solution.py:106
  34.1 0.1 pad_maximum_fusion.1
  34.2 0.8 %bitcast_convert_fusion.1.ext_p = f32[768,128]{1,0:T(8,128)} fusion(bf16[4,4,6,8,128]{4,3,2,1,0:T(8,128)(2,1)S(1)} %pad_maximum_fusion.1), kind=kLoop, calls=%fused_computation.5 | loop fusion | flops 98304 | bytes 589824 | tf_op jit(solution)/shard_map/convert_element_type | solution.py:224
  35.0 0.0 copy-start.2
  35.0 0.2 pad_maximum_fusion
  35.2 1.3 %bitcast_convert_fusion.ext_f = f32[2880,128]{1,0:T(8,128)} fusion(bf16[6,6,10,8,128]{4,3,2,1,0:T(8,128)(2,1)S(1)} %pad_maximum_fusion), kind=kLoop, calls=%fused_computation.1 | loop fusion | flops 368640 | bytes 2211840 | tf_op jit(solution)/shard_map/convert_element_type | solution.py:224
  36.5 0.0 copy-done.2
  36.5 0.7 jit_solution_.3.bits
  37.2 37.5 %interact.1 = (bf16[1024,128]{1,0:T(8,128)(2,1)}, bf16[128,128]{1,0:T(8,128)(2,1)}) custom-call(s32[2528]{0:T(1024)} %constant.5.clone.wtab, f32[2880,128]{1,0:T(8,128)} %bitcast_convert_fusion.ext_f, f32[768,128]{1,0:T(8,128)} %bitcast_convert_fusion.1.ext_p, s32[8,144,20]{2,1,0:T(8,128)} %pad_add_fusion.words, s16[16,16,128]{2,1,0:T(8,128)(2,1)} %jit_solution_.3.bits, ...), custom_call_target="tpu_custom_call" | custom-call | flops 7134511104 | bytes 10354688 | tf_op jit(solution)/shard_map/interact/pallas_call | solution.py:239
  (28 shorter events, 0.3 us)
Async XLA Ops:
  0.6 20.4 %copy-start = (s32[20,1024]{1,0:T(8,128)S(1)}, s32[20,1024]{1,0:T(8,128)}, u32[]{:S(2)}) copy-start(s32[20,1024]{1,0:T(8,128)} %param.10) | copy-start | bytes 245764
  2.4 6.9 %collective-permute-start = (bf16[40,8,128]{2,1,0:T(8,128)(2,1)S(1)}, bf16[40,8,128]{2,1,0:T(8,128)(2,1)S(1)}, u32[]{:S(2)}, u32[]{:S(2)}) collective-permute-start(bf16[40,8,128]{2,1,0:T(8,128)(2,1)S(1)} %pad_maximum_fusion.9), channel_id=1, source_target_pairs={{0,2},{1,3},{2,16},{3,17},{4,6},{5,7},{6,20},{7,21},{8,10},{9,11},... | collective-permute-start | bytes 245768 | tf_op jit(solution)/shard_map/ppermute | solution.py:106
  6.7 7.0 %collective-permute-start.1 = (bf16[40,8,128]{2,1,0:T(8,128)(2,1)S(1)}, bf16[40,8,128]{2,1,0:T(8,128)(2,1)S(1)}, u32[]{:S(2)}, u32[]{:S(2)}) collective-permute-start(bf16[40,8,128]{2,1,0:T(8,128)(2,1)S(1)} %pad_maximum_fusion.10), channel_id=1, source_target_pairs={{2,0},{3,1},{6,4},{7,5},{10,8},{11,9},{14,12},{15,13},{16,2},{17,3... | collective-permute-start | bytes 245768 | tf_op jit(solution)/shard_map/ppermute | solution.py:106
  13.8 7.8 %collective-permute-start.2 = (bf16[64,8,128]{2,1,0:T(8,128)(2,1)S(1)}, bf16[64,8,128]{2,1,0:T(8,128)(2,1)S(1)}, u32[]{:S(2)}, u32[]{:S(2)}) collective-permute-start(bf16[64,8,128]{2,1,0:T(8,128)(2,1)S(1)} %pad_maximum_fusion.2), channel_id=1, source_target_pairs={{0,1},{1,8},{2,3},{3,10},{4,5},{5,12},{6,7},{7,14},{8,9},{10,11},{... | collective-permute-start | bytes 393224 | tf_op jit(solution)/shard_map/ppermute | solution.py:106
  19.1 2.4 %copy-start.1 = (s32[20,128]{1,0:T(8,128)S(1)}, s32[20,128]{1,0:T(8,128)}, u32[]{:S(2)}) copy-start(s32[20,128]{1,0:T(8,128)} %param.11) | copy-start | bytes 30724
  19.1 6.3 %collective-permute-start.3 = (bf16[64,8,128]{2,1,0:T(8,128)(2,1)S(1)}, bf16[64,8,128]{2,1,0:T(8,128)(2,1)S(1)}, u32[]{:S(2)}, u32[]{:S(2)}) collective-permute-start(bf16[64,8,128]{2,1,0:T(8,128)(2,1)S(1)} %pad_maximum_fusion.3), channel_id=1, source_target_pairs={{1,0},{3,2},{5,4},{7,6},{8,1},{9,8},{10,3},{11,10},{12,5},{13,12},... | collective-permute-start | bytes 393224 | tf_op jit(solution)/shard_map/ppermute | solution.py:106
  25.5 5.4 %collective-permute-start.4 = (bf16[52,8,128]{2,1,0:T(8,128)(2,1)S(1)}, bf16[52,8,128]{2,1,0:T(8,128)(2,1)S(1)}, u32[]{:S(2)}, u32[]{:S(2)}) collective-permute-start(bf16[52,8,128]{2,1,0:T(8,128)(2,1)S(1)} %pad_maximum_fusion.4), channel_id=1, source_target_pairs={{0,4},{1,5},{2,6},{3,7},{8,12},{9,13},{10,14},{11,15},{16,20},{17,... | collective-permute-start | bytes 319496 | tf_op jit(solution)/shard_map/ppermute | solution.py:106
  28.7 5.4 %collective-permute-start.5 = (bf16[52,8,128]{2,1,0:T(8,128)(2,1)S(1)}, bf16[52,8,128]{2,1,0:T(8,128)(2,1)S(1)}, u32[]{:S(2)}, u32[]{:S(2)}) collective-permute-start(bf16[52,8,128]{2,1,0:T(8,128)(2,1)S(1)} %pad_maximum_fusion.5), channel_id=1, source_target_pairs={{4,0},{5,1},{6,2},{7,3},{12,8},{13,9},{14,10},{15,11},{20,16},{21,... | collective-permute-start | bytes 319496 | tf_op jit(solution)/shard_map/ppermute | solution.py:106
  35.0 1.5 %copy-start.2 = (s16[16]{0:T(256)(128)(2,1)S(1)}, s16[16]{0:T(256)(128)(2,1)}, u32[]{:S(2)}) copy-start(s16[16]{0:T(256)(128)(2,1)} %constant.4.clone) | copy-start | bytes 100

commit v2 on v1

--- a/solution.py
+++ b/solution.py
@@ -79,42 +79,92 @@
     return (coords[0] * extents[1] + coords[1]) * extents[2] + coords[2]
 
 
-def shift_route(count, level_bits, dim, step):
-    bits = count.bit_length() - 1
-    owned = [k for k in range(bits) if 2 - (level_bits + k) % 3 == dim]
-    route = []
-    for src in range(count):
-        at = sum((src >> k & 1) << n for n, k in enumerate(owned)) + step
-        if 0 <= at < 2 ** len(owned):
-            dst = src
-            for n, k in enumerate(owned):
-                dst = dst & ~(1 << k) | (at >> n & 1) << k
-            route.append((src, dst))
-    return route
-
-
-def extend(blocks, level_bits, count):
+def halo_kernel(count, level_bits, fext, gext, fine, parent, out_f, out_p, ext_f, ext_p, sent, got):
+    me = lax.axis_index("box")
+    levels = ((fine, ext_f, fext), (parent, ext_p, gext))
+    for _, ext, _ in levels:
+        ext[...] = jnp.zeros_like(ext)
+    for block, ext, (sx, sy, sz) in levels:
+        for m in range(sx * sy * sz):
+            at = grid_index(m, (sx, sy, sz))
+            ext[1 + at // (sy * sz), 1 + at // sz % sy, 1 + at % sz] = block[m]
+
+    around = []
     for dim in range(3):
-        halos = []
+        owned = [k for k in range(count.bit_length() - 1) if 2 - (level_bits + k) % 3 == dim]
+        at = sum((me // 2**k % 2) * 2**n for n, k in enumerate(owned))
+        base = me - sum((me // 2**k % 2) * 2**k for k in owned)
+        sides = []
         for step in (1, -1):
-            faces = []
-            for block in blocks:
-                size = block.shape[dim]
-                start = size - 1 if step == 1 else 0
-                faces.append(lax.slice_in_dim(block, start, start + 1, axis=dim))
-            flat = jnp.concatenate([f.reshape((-1,) + f.shape[3:]) for f in faces])
-            got = lax.ppermute(flat, "box", shift_route(count, level_bits, dim, step))
-            parts, row = [], 0
-            for f in faces:
-                rows = f.shape[0] * f.shape[1] * f.shape[2]
-                parts.append(got[row : row + rows].reshape(f.shape))
-                row += rows
-            halos.append(parts)
-        blocks = [
-            jnp.concatenate([low, block, high], axis=dim)
-            for low, block, high in zip(halos[0], blocks, halos[1])
-        ]
-    return blocks
+            to = at + step + 2 ** len(owned)
+            dst = base + sum((to // 2**n % 2) * 2**k for n, k in enumerate(owned))
+            inside = at < 2 ** len(owned) - 1 if step == 1 else at > 0
+            sides.append((inside, dst))
+        around.append(sides)
+
+    barrier = pltpu.get_barrier_semaphore()
+    for sides in around:
+        for inside, dst in sides:
+            @pl.when(inside)
+            def _(dst=dst):
+                pl.semaphore_signal(
+                    barrier, inc=1, device_id=(dst,), device_id_type=pl.DeviceIdType.MESH
+                )
+    peers = sum(inside.astype(jnp.int32) for sides in around for inside, _ in sides)
+    pl.semaphore_wait(barrier, peers)
+
+    for dim in range(3):
+        copies = []
+        for level, (_, ext, size) in enumerate(levels):
+            for side in range(2):
+                rest = [
+                    pl.ds(0, size[k] + 2) if k < dim else pl.ds(1, size[k]) for k in range(3)
+                ]
+                src, dst = list(rest), list(rest)
+                src[dim] = pl.ds(size[dim] if side == 0 else 1, 1)
+                dst[dim] = pl.ds(0 if side == 0 else size[dim] + 1, 1)
+                copy = pltpu.make_async_remote_copy(
+                    src_ref=ext.at[tuple(src)],
+                    dst_ref=ext.at[tuple(dst)],
+                    send_sem=sent.at[dim, level, side],
+                    recv_sem=got.at[dim, level, side],
+                    device_id=(around[dim][side][1],),
+                    device_id_type=pl.DeviceIdType.MESH,
+                )
+                copies.append((copy, around[dim][side][0], around[dim][1 - side][0]))
+        for copy, to, source in copies:
+            pl.when(to)(copy.start)
+        for copy, to, source in copies:
+            pl.when(source)(copy.wait_recv)
+        for copy, to, source in copies:
+            pl.when(to)(copy.wait_send)
+
+    for ext, out, size in ((ext_f, out_f, fext), (ext_p, out_p, gext)):
+        line = (size[2] + 2) * 8
+        for x in range(size[0] + 2):
+            for y in range(size[1] + 2):
+                rows = ext[x, y].astype(jnp.float32).reshape(line, ext.shape[4])
+                out[pl.ds((x * (size[1] + 2) + y) * line, line), :] = rows
+
+
+def exchange(fine_mult, parent_mult, fbits, fext, gext):
+    count, width = lax.axis_size("box"), fine_mult.shape[1]
+    wide = [tuple(e + 2 for e in ext) for ext in (fext, gext)]
+    vmem = pl.BlockSpec(memory_space=pltpu.VMEM)
+    return pl.pallas_call(
+        functools.partial(halo_kernel, count, fbits + 3, fext, gext),
+        out_shape=[
+            jax.ShapeDtypeStruct((w[0] * w[1] * w[2] * 8, width), jnp.float32) for w in wide
+        ],
+        in_specs=[vmem, vmem],
+        out_specs=[vmem, vmem],
+        scratch_shapes=[pltpu.VMEM(w + (8, width), jnp.bfloat16) for w in wide]
+        + [pltpu.SemaphoreType.DMA((3, 2, 2)), pltpu.SemaphoreType.DMA((3, 2, 2))],
+        compiler_params=pltpu.CompilerParams(
+            collective_id=0, has_side_effects=True, vmem_limit_bytes=32 * 1024 * 1024
+        ),
+        name="halo",
+    )(fine_mult.reshape(-1, 8, width), parent_mult.reshape(-1, 8, width))
 
 
 def interact_kernel(
@@ -208,7 +258,6 @@
 
 
 def on_device(fine_mult, parent_mult, fine_mask, parent_mask, kernels, shift_ops):
-    count = lax.axis_size("box")
     width = fine_mult.shape[1]
     fbits = fine_mult.shape[0].bit_length() - 4
     pbits = parent_mult.shape[0].bit_length() - 4
@@ -216,13 +265,7 @@
     nf, ng = 2**fbits, 2**pbits
     rows = nf + ng
 
-    blocks = [
-        to_grid(fine_mult.reshape(nf, 8, width), fbits),
-        to_grid(parent_mult.reshape(ng, 8, width), pbits),
-    ]
-    ext_f, ext_p = (
-        b.reshape(-1, width).astype(jnp.float32) for b in extend(blocks, fbits + 3, count)
-    )
+    ext_f, ext_p = exchange(fine_mult, parent_mult, fbits, fext, gext)
 
     def by_class(mask, bits, total):
         grid = to_grid(jnp.transpose(mask).reshape(total, 8, 20), bits)

time: 75.1 us -> 62.4 us (0.83)
  starting transfers between devices: 17.8 us -> 0 us
  Pallas kernels: 37.5 us -> 52.9 us
  waiting for transfers between devices: 11.3 us -> 0 us
  local copies, waits for them, and re-layouts: 3.82 us -> 7.04 us
  other arithmetic: 3.31 us -> 0.86 us
    ppermute x6 -> x0, starting transfers between devices: 17.8 us -> none  [extend(): got = lax.ppermute(flat, 'box', shift_route(count, level_bits, dim, step))]
    pallas_call x0 -> x1, Pallas kernels: none -> 15.4 us  [exchange(): pl.pallas_call(functools.partial(halo_kernel, count, fbits + 3, fext, gex...]
    ppermute x6 -> x0, waiting for transfers between devices: 11.3 us -> none  [extend(): got = lax.ppermute(flat, 'box', shift_route(count, level_bits, dim, step))]
    unnamed x8 -> x10, local copies, waits for them, and re-layouts: 0.34 us -> 5.49 us
    convert_element_type x2 -> x0, other arithmetic: 2.04 us -> none  [on_device(): b.reshape(-1, width).astype(jnp.float32)]
    transpose x4 -> x2, local copies, waits for them, and re-layouts: 1.83 us -> 0.06 us  [to_grid(): jnp.transpose(bitwise, tuple(order) + kept)]
    slice x17 -> x0, local copies, waits for them, and re-layouts: 0.83 us -> none  [the longest x5 0.77 us: extend(): faces.append(lax.slice_in_dim(block, start, start + 1, axis=dim))]
  transfers between devices with their start and end apart: 6 -> 0, of which waited for: 3 -> 0; matrix products, arithmetic and copies ran while one was open for 3% -> 0% of each run, Pallas kernels for 0% -> 0%
where the time goes in v2:
time: 62.4 us; the launch traced here: 61.5 us
  Pallas kernels  52.9 us (85%)
  local copies, waits for them, and re-layouts  7.04 us (11%)
  other arithmetic  0.86 us (1%)
  between operations  0.69 us (1%)
    pallas_call x1, Pallas kernels, on_device(): pl.pallas_call(functools.partial(interact_kernel, fext, gext), out_shape=...  37.5 us
    pallas_call x1, Pallas kernels, exchange(): pl.pallas_call(functools.partial(halo_kernel, count, fbits + 3, fext, gex...  15.4 us
    unnamed x10, local copies, waits for them, and re-layouts  5.49 us
    another operation x1, local copies, waits for them, and re-layouts  1.37 us

profile of v2, /device:TPU:3, one launch (start us, length us, event | category | flops | bytes accessed | tf_op | source)
XLA Modules:
  0.0 61.5 jit_solution(15941448049858761031)
XLA Ops:
  0.6 0.8 %copy.29 = s32[20,128]{0,1:T(8,128)S(1)} copy(s32[20,128]{1,0:T(8,128)} %param.11) | data formatting | bytes 20480 | tf_op args[3]
  1.5 1.1 %copy.26 = s32[20,1024]{0,1:T(8,128)S(1)} copy(s32[20,1024]{1,0:T(8,128)} %param.10) | data formatting | bytes 163840 | tf_op args[2]
  2.6 0.1 copy.27
  2.6 0.1 copy.34
  2.8 0.9 %pad_add_fusion.words = s32[8,144,20]{2,1,0:T(8,128)} fusion(s32[8,16,20]{2,1,0:T(8,128)S(1)} %bitcast.25, s32[8,128,20]{2,1,0:T(8,128)S(1)} %bitcast.22), kind=kLoop, calls=%fused_computation | loop fusion | flops 23040 | bytes 184320 | tf_op jit(solution)/shard_map/concatenate | solution.py:274
  3.6 0.0 copy-start
  3.6 0.9 %copy-done = bf16[1024,128]{1,0:T(8,128)(2,1)S(1)} copy-done((bf16[1024,128]{1,0:T(8,128)(2,1)S(1)}, bf16[1024,128]{1,0:T(8,128)(2,1)}, u32[]{:S(2)}) %copy-start) | copy-done | bytes 262168
  4.6 0.0 copy-start.1
  4.6 0.8 %copy-done.1 = bf16[128,128]{1,0:T(8,128)(2,1)S(1)} copy-done((bf16[128,128]{1,0:T(8,128)(2,1)S(1)}, bf16[128,128]{1,0:T(8,128)(2,1)}, u32[]{:S(2)}) %copy-start.1) | copy-done | bytes 32792
  5.3 15.4 %halo.1 = (f32[2880,128]{1,0:T(8,128)S(1)}, f32[768,128]{1,0:T(8,128)S(1)}) custom-call(bf16[128,8,128]{2,1,0:T(8,128)(2,1)S(1)} %bitcast.20, bf16[16,8,128]{2,1,0:T(8,128)(2,1)S(1)} %bitcast.21), custom_call_target="tpu_custom_call" | custom-call | tf_op jit(solution)/shard_map/halo/pallas_call | solution.py:154
  20.8 0.0 copy-start.2
  20.8 1.1 %copy-done.2 = f32[2880,128]{1,0:T(8,128)} copy-done((f32[2880,128]{1,0:T(8,128)}, f32[2880,128]{1,0:T(8,128)S(1)}, u32[]{:S(2)}) %copy-start.2) | copy-done | bytes 1474584
  21.9 0.0 copy-start.3
  21.9 0.7 %copy-done.3 = f32[768,128]{1,0:T(8,128)} copy-done((f32[768,128]{1,0:T(8,128)}, f32[768,128]{1,0:T(8,128)S(1)}, u32[]{:S(2)}) %copy-start.3) | copy-done | bytes 393240
  22.6 1.4 %jit_solution_.3.bits = s16[16,16,128]{2,1,0:T(8,128)(2,1)} broadcast(s16[16]{0:T(256)(128)(2,1)} %constant.4.clone), dimensions={0} | broadcast | bytes 65568 | tf_op jit(solution)
  24.0 37.5 %interact.1 = (bf16[1024,128]{1,0:T(8,128)(2,1)}, bf16[128,128]{1,0:T(8,128)(2,1)}) custom-call(s32[2528]{0:T(1024)} %constant.5.clone.wtab, f32[2880,128]{1,0:T(8,128)} %copy-done.2, f32[768,128]{1,0:T(8,128)} %copy-done.3, s32[8,144,20]{2,1,0:T(8,128)} %pad_add_fusion.words, s16[16,16,128]{2,1,0:T(8,128)(2,1)} %jit_solution_.3.bits, ...), custom_call_target="tpu_custom_call" | custom-call | flops 7134511104 | bytes 10354688 | tf_op jit(solution)/shard_map/interact/pallas_call | solution.py:282
  (2 shorter events, 0.0 us)
Async XLA Ops:
  3.6 0.9 %copy-start = (bf16[1024,128]{1,0:T(8,128)(2,1)S(1)}, bf16[1024,128]{1,0:T(8,128)(2,1)}, u32[]{:S(2)}) copy-start(bf16[1024,128]{1,0:T(8,128)(2,1)} %param.8) | copy-start | bytes 786436
  4.6 0.8 %copy-start.1 = (bf16[128,128]{1,0:T(8,128)(2,1)S(1)}, bf16[128,128]{1,0:T(8,128)(2,1)}, u32[]{:S(2)}) copy-start(bf16[128,128]{1,0:T(8,128)(2,1)} %param.9) | copy-start | bytes 98308
  20.8 1.1 %copy-start.2 = (f32[2880,128]{1,0:T(8,128)}, f32[2880,128]{1,0:T(8,128)S(1)}, u32[]{:S(2)}) copy-start(f32[2880,128]{1,0:T(8,128)S(1)} %get-tuple-element.4.ext_f) | copy-start | bytes 4423684
  21.9 0.7 %copy-start.3 = (f32[768,128]{1,0:T(8,128)}, f32[768,128]{1,0:T(8,128)S(1)}, u32[]{:S(2)}) copy-start(f32[768,128]{1,0:T(8,128)S(1)} %get-tuple-element.5.ext_p) | copy-start | bytes 1179652

commit v3 on v2

--- a/solution.py
+++ b/solution.py
@@ -79,7 +79,10 @@
     return (coords[0] * extents[1] + coords[1]) * extents[2] + coords[2]
 
 
-def halo_kernel(count, level_bits, fext, gext, fine, parent, out_f, out_p, ext_f, ext_p, sent, got):
+def halo_kernel(
+    count, level_bits, fext, gext, fine, parent, fmask, pmask, out_f, out_p, wb,
+    ext_f, ext_p, turned_f, turned_p, sent, got,
+):
     me = lax.axis_index("box")
     levels = ((fine, ext_f, fext), (parent, ext_p, gext))
     for _, ext, _ in levels:
@@ -112,6 +115,28 @@
                 )
     peers = sum(inside.astype(jnp.int32) for sides in around for inside, _ in sides)
     pl.semaphore_wait(barrier, peers)
+
+    nf, ng = fext[0] * fext[1] * fext[2], gext[0] * gext[1] * gext[2]
+    rows = nf + ng
+
+    def turn(mask, turned, ext):
+        boxes = mask.shape[1]
+        for first in range(0, boxes, 128):
+            block = jnp.concatenate(
+                [mask[:16, first : first + 128], mask[16:, first : first + 128],
+                 jnp.zeros((108, 128), jnp.int32)], axis=0,
+            ).T
+            for k in range(16):
+                at = grid_index(first // 8 + k, ext)
+                turned[pl.ds(at * 8, 8), :] = block[k * 8 : k * 8 + 8]
+
+    def spread(c):
+        mine = jnp.concatenate(
+            [turned_f[pl.ds(c, nf, stride=8), :], turned_p[pl.ds(c, ng, stride=8), :]], axis=0
+        )
+        for w in range(20):
+            wide = jnp.broadcast_to(mine[:, w : w + 1], (rows, 128)).astype(jnp.int16)
+            wb[c, w] = wide.reshape(rows // 16, 16, 128)
 
     for dim in range(3):
         copies = []
@@ -134,6 +159,11 @@
                 copies.append((copy, around[dim][side][0], around[dim][1 - side][0]))
         for copy, to, source in copies:
             pl.when(to)(copy.start)
+        if dim == 0:
+            turn(fmask, turned_f, fext)
+            turn(pmask, turned_p, gext)
+        for c in ((0, 1), (2, 3, 4), (5, 6, 7))[dim]:
+            spread(c)
         for copy, to, source in copies:
             pl.when(source)(copy.wait_recv)
         for copy, to, source in copies:
@@ -147,62 +177,61 @@
                 out[pl.ds((x * (size[1] + 2) + y) * line, line), :] = rows
 
 
-def exchange(fine_mult, parent_mult, fbits, fext, gext):
+def exchange(fine_mult, parent_mult, fine_mask, parent_mask, fbits, fext, gext):
     count, width = lax.axis_size("box"), fine_mult.shape[1]
     wide = [tuple(e + 2 for e in ext) for ext in (fext, gext)]
+    boxes = [fine_mult.shape[0], parent_mult.shape[0]]
     vmem = pl.BlockSpec(memory_space=pltpu.VMEM)
     return pl.pallas_call(
         functools.partial(halo_kernel, count, fbits + 3, fext, gext),
         out_shape=[
             jax.ShapeDtypeStruct((w[0] * w[1] * w[2] * 8, width), jnp.float32) for w in wide
-        ],
-        in_specs=[vmem, vmem],
-        out_specs=[vmem, vmem],
+        ] + [jax.ShapeDtypeStruct((8, 20, sum(boxes) // 128, 16, width), jnp.int16)],
+        in_specs=[vmem] * 4,
+        out_specs=[vmem] * 3,
         scratch_shapes=[pltpu.VMEM(w + (8, width), jnp.bfloat16) for w in wide]
+        + [pltpu.VMEM((b, 128), jnp.int32) for b in boxes]
         + [pltpu.SemaphoreType.DMA((3, 2, 2)), pltpu.SemaphoreType.DMA((3, 2, 2))],
         compiler_params=pltpu.CompilerParams(
-            collective_id=0, has_side_effects=True, vmem_limit_bytes=32 * 1024 * 1024
+            collective_id=0, has_side_effects=True, vmem_limit_bytes=24 * 1024 * 1024
         ),
         name="halo",
-    )(fine_mult.reshape(-1, 8, width), parent_mult.reshape(-1, 8, width))
+    )(
+        fine_mult.reshape(-1, 8, width), parent_mult.reshape(-1, 8, width), fine_mask, parent_mask
+    )
 
 
 def interact_kernel(
-    fext, gext, wtab, ext_f, ext_p, words, bits, shift, kernels,
-    fine_out, parent_out, kv, win, wb, acc, acc_f, acc_p, par, sem,
+    fext, gext, wtab, ext_f, ext_p, wb, shift_ops, kernels,
+    fine_out, parent_out, kv, win, shift, bits, acc, acc_f, acc_p, par, sem,
 ):
     nf, ng = fext[0] * fext[1] * fext[2], gext[0] * gext[1] * gext[2]
     rows = nf + ng
     tiles = rows // 16
-    fetch = pltpu.make_async_copy(kernels, kv, sem)
+    fetch = pltpu.make_async_copy(kernels, kv, sem.at[0])
     fetch.start()
-
-    def build(index, carry):
-        delta, source = index // 8, index % 8
+    fetch_shift = pltpu.make_async_copy(shift_ops, shift, sem.at[1])
+    fetch_shift.start()
+    for k in range(16):
+        bits[k] = jnp.full((16, 128), 1 << k if k < 15 else -(1 << 15), jnp.int16)
+    acc[...] = jnp.zeros_like(acc)
+
+    def build(delta, carry):
         dx, dy, dz = delta // 9, delta // 3 % 3, delta % 3
         for ref, ext, base in ((ext_f, fext, 0), (ext_p, gext, nf)):
-            got = []
-            for x in range(ext[0]):
-                for y in range(ext[1]):
-                    first = ((x + dx) * (ext[1] + 2) + y + dy) * (ext[2] + 2) + dz
-                    got.append(ref[pl.ds(first * 8 + source, ext[2], stride=8), :])
-            stack = jnp.concatenate(got, axis=0).astype(jnp.bfloat16)
-            count = stack.shape[0] // 16
-            win[index, pl.ds(base // 16, count)] = stack.reshape(count, 16, 128)
+            for source in range(8):
+                got = []
+                for x in range(ext[0]):
+                    for y in range(ext[1]):
+                        first = ((x + dx) * (ext[1] + 2) + y + dy) * (ext[2] + 2) + dz
+                        got.append(ref[pl.ds(first * 8 + source, ext[2], stride=8), :])
+                stack = jnp.concatenate(got, axis=0).astype(jnp.bfloat16)
+                count = stack.shape[0] // 16
+                win[delta * 8 + source, pl.ds(base // 16, count)] = stack.reshape(count, 16, 128)
         return carry
 
-    lax.fori_loop(0, 216, build, 0)
+    lax.fori_loop(0, 27, build, 0)
     fetch.wait()
-
-    def spread(c, carry):
-        mine = words[c]
-        for w in range(20):
-            wide = jnp.broadcast_to(mine[:, w : w + 1], (rows, 128)).astype(jnp.int16)
-            wb[c, w] = wide.reshape(tiles, 16, 128)
-        acc[c] = jnp.zeros((rows, 128), jnp.float32)
-        return carry
-
-    lax.fori_loop(0, 8, spread, 0)
 
     def contract(start, count, classes):
         lhs = []
@@ -245,6 +274,7 @@
                 to = ((2 * gx + cx) * fext[1] + 2 * gy + cy) * fext[2] + cz
                 par[pl.ds(to, gext[2], stride=2), :] = acc_p[pl.ds(first, gext[2]), :]
     local = par[...].astype(jnp.bfloat16)
+    fetch_shift.wait()
     for c in range(8):
         acc_f[pl.ds(c * nf, nf), :] += jnp.dot(
             local, shift[c], preferred_element_type=jnp.float32
@@ -265,19 +295,12 @@
     nf, ng = 2**fbits, 2**pbits
     rows = nf + ng
 
-    ext_f, ext_p = exchange(fine_mult, parent_mult, fbits, fext, gext)
-
-    def by_class(mask, bits, total):
-        grid = to_grid(jnp.transpose(mask).reshape(total, 8, 20), bits)
-        return jnp.transpose(grid.reshape(total, 8, 20), (1, 0, 2))
-
-    words = jnp.concatenate(
-        [by_class(fine_mask, fbits, nf), by_class(parent_mask, pbits, ng)], axis=1
+    ext_f, ext_p, wb = exchange(
+        fine_mult, parent_mult, fine_mask, parent_mask, fbits, fext, gext
     )
     wtab = window_table()
-    flags = np.array([1 << k if k < 15 else -(1 << 15) for k in range(16)], np.int16)
-    bits = np.broadcast_to(flags[:, None, None], (16, 16, 128))
     smem = pl.BlockSpec(memory_space=pltpu.SMEM)
+    hbm = pl.BlockSpec(memory_space=pl.ANY)
     vmem = pl.BlockSpec(memory_space=pltpu.VMEM)
     return pl.pallas_call(
         functools.partial(interact_kernel, fext, gext),
@@ -285,26 +308,27 @@
             jax.ShapeDtypeStruct(fine_mult.shape, jnp.bfloat16),
             jax.ShapeDtypeStruct(parent_mult.shape, jnp.bfloat16),
         ],
-        in_specs=[smem, vmem, vmem, vmem, vmem, vmem, pl.BlockSpec(memory_space=pl.ANY)],
+        in_specs=[smem, vmem, vmem, vmem, hbm, hbm],
         out_specs=[vmem, vmem],
         scratch_shapes=[
             pltpu.VMEM(kernels.shape, jnp.bfloat16),
             pltpu.VMEM((216, rows // 16, 16, width), jnp.bfloat16),
-            pltpu.VMEM((8, 20, rows // 16, 16, width), jnp.int16),
+            pltpu.VMEM(shift_ops.shape, jnp.bfloat16),
+            pltpu.VMEM((16, 16, width), jnp.int16),
             pltpu.VMEM((8, rows, width), jnp.float32),
             pltpu.VMEM((8 * nf, width), jnp.float32),
             pltpu.VMEM((8 * ng, width), jnp.float32),
             pltpu.VMEM((nf, width), jnp.float32),
-            pltpu.SemaphoreType.DMA,
+            pltpu.SemaphoreType.DMA((2,)),
         ],
-        compiler_params=pltpu.CompilerParams(vmem_limit_bytes=56 * 1024 * 1024),
+        compiler_params=pltpu.CompilerParams(vmem_limit_bytes=44 * 1024 * 1024),
         cost_estimate=pl.CostEstimate(
             flops=2 * 8 * rows * 189 * width * width,
             bytes_accessed=kernels.size * 2,
             transcendentals=0,
         ),
         name="interact",
-    )(wtab, ext_f, ext_p, words, jnp.asarray(bits), shift_ops, kernels)
+    )(wtab, ext_f, ext_p, wb, shift_ops, kernels)
 
 
 def solution(mesh):

time: 62.4 us -> 49.2 us (0.79)
  Pallas kernels: 52.9 us -> 42.7 us
  local copies, waits for them, and re-layouts: 7.04 us -> 4.95 us
  other arithmetic: 0.86 us -> 0 us
    pallas_call x1, Pallas kernels: 37.5 us -> 26.9 us  [on_device(): pl.pallas_call(functools.partial(interact_kernel, fext, gext), out_shape=...]
    another operation x3 -> x0, local copies, waits for them, and re-layouts: 1.49 us -> none
    concatenate x1 -> x0, other arithmetic: 0.86 us -> none  [on_device(): jnp.concatenate([by_class(fine_mask, fbits, nf), by_class(parent_mask, pb...]
    unnamed x10 -> x12, local copies, waits for them, and re-layouts: 5.49 us -> 4.95 us
where the time goes in v3:
time: 49.2 us; the launch traced here: 48.5 us
  Pallas kernels  42.7 us (87%)
  local copies, waits for them, and re-layouts  4.95 us (10%)
  between operations  0.82 us (2%)
    pallas_call x1, Pallas kernels, on_device(): pl.pallas_call(functools.partial(interact_kernel, fext, gext), out_shape=...  26.9 us
    pallas_call x1, Pallas kernels, exchange(): pl.pallas_call(functools.partial(halo_kernel, count, fbits + 3, fext, gex...  15.9 us
    unnamed x12, local copies, waits for them, and re-layouts  4.95 us

profile of v3, /device:TPU:3, one launch (start us, length us, event | category | flops | bytes accessed | tf_op | source)
XLA Modules:
  0.0 48.5 jit_solution(6869787494426470126)
XLA Ops:
  0.6 0.0 copy-start
  0.6 0.9 %copy-done = bf16[1024,128]{1,0:T(8,128)(2,1)S(1)} copy-done((bf16[1024,128]{1,0:T(8,128)(2,1)S(1)}, bf16[1024,128]{1,0:T(8,128)(2,1)}, u32[]{:S(2)}) %copy-start) | copy-done | bytes 262168
  1.6 0.0 copy-start.1
  1.6 0.9 %copy-done.1 = s32[20,1024]{1,0:T(8,128)S(1)} copy-done((s32[20,1024]{1,0:T(8,128)S(1)}, s32[20,1024]{1,0:T(8,128)}, u32[]{:S(2)}) %copy-start.1) | copy-done | bytes 81944
  2.5 0.0 copy-start.2
  2.5 0.8 %copy-done.2 = bf16[128,128]{1,0:T(8,128)(2,1)S(1)} copy-done((bf16[128,128]{1,0:T(8,128)(2,1)S(1)}, bf16[128,128]{1,0:T(8,128)(2,1)}, u32[]{:S(2)}) %copy-start.2) | copy-done | bytes 32792
  3.2 0.0 copy-start.3
  3.2 0.7 %copy-done.3 = s32[20,128]{1,0:T(8,128)S(1)} copy-done((s32[20,128]{1,0:T(8,128)S(1)}, s32[20,128]{1,0:T(8,128)}, u32[]{:S(2)}) %copy-start.3) | copy-done | bytes 10264
  3.9 15.9 %halo.1 = (f32[2880,128]{1,0:T(8,128)S(1)}, f32[768,128]{1,0:T(8,128)S(1)}, s16[8,20,9,16,128]{4,3,2,1,0:T(8,128)(2,1)S(1)}) custom-call(bf16[128,8,128]{2,1,0:T(8,128)(2,1)S(1)} %bitcast.2, bf16[16,8,128]{2,1,0:T(8,128)(2,1)S(1)} %bitcast.3, s32[20,1024]{1,0:T(8,128)S(1)} %copy-done.1, s32[20,128]{1,0:T(8,128)S(1)} %copy-done.3), custom_call_target="tpu_custom_call" | custom-call | tf_op jit(solution)/shard_map/halo/pallas_call | solution.py:185
  19.8 0.0 copy-start.4
  19.8 0.9 %copy-done.4 = bf16[8,128,128]{2,1,0:T(8,128)(2,1)S(1)} copy-done((bf16[8,128,128]{2,1,0:T(8,128)(2,1)S(1)}, bf16[8,128,128]{2,1,0:T(8,128)(2,1)}, u32[]{:S(2)}) %copy-start.4) | copy-done | bytes 262168
  20.8 0.0 copy-start.5
  20.8 0.7 %copy-done.5 = s32[2528]{0:T(1024)S(1)} copy-done((s32[2528]{0:T(1024)S(1)}, s32[2528]{0:T(1024)}, u32[]{:S(2)}) %copy-start.5) | copy-done | bytes 10136
  21.5 26.9 %interact.1 = (bf16[1024,128]{1,0:T(8,128)(2,1)}, bf16[128,128]{1,0:T(8,128)(2,1)}) custom-call(s32[2528]{0:T(1024)S(1)} %copy-done.5, f32[2880,128]{1,0:T(8,128)S(1)} %get-tuple-element.5.ext_f, f32[768,128]{1,0:T(8,128)S(1)} %get-tuple-element.6.ext_p, s16[8,20,9,16,128]{4,3,2,1,0:T(8,128)(2,1)S(1)} %get-tuple-element.7.wb, ...), custom_call_target="tpu_custom_call" | custom-call | flops 7134511104 | bytes 10354688 | tf_op jit(solution)/shard_map/interact/pallas_call | solution.py:305
Async XLA Ops:
  0.6 1.0 %copy-start = (bf16[1024,128]{1,0:T(8,128)(2,1)S(1)}, bf16[1024,128]{1,0:T(8,128)(2,1)}, u32[]{:S(2)}) copy-start(bf16[1024,128]{1,0:T(8,128)(2,1)} %param.7) | copy-start | bytes 786436
  1.6 0.9 %copy-start.1 = (s32[20,1024]{1,0:T(8,128)S(1)}, s32[20,1024]{1,0:T(8,128)}, u32[]{:S(2)}) copy-start(s32[20,1024]{1,0:T(8,128)} %fmask.1) | copy-start | bytes 245764
  2.5 0.8 %copy-start.2 = (bf16[128,128]{1,0:T(8,128)(2,1)S(1)}, bf16[128,128]{1,0:T(8,128)(2,1)}, u32[]{:S(2)}) copy-start(bf16[128,128]{1,0:T(8,128)(2,1)} %param.8) | copy-start | bytes 98308
  3.2 0.7 %copy-start.3 = (s32[20,128]{1,0:T(8,128)S(1)}, s32[20,128]{1,0:T(8,128)}, u32[]{:S(2)}) copy-start(s32[20,128]{1,0:T(8,128)} %pmask.1) | copy-start | bytes 30724
  19.8 1.0 %copy-start.4 = (bf16[8,128,128]{2,1,0:T(8,128)(2,1)S(1)}, bf16[8,128,128]{2,1,0:T(8,128)(2,1)}, u32[]{:S(2)}) copy-start(bf16[8,128,128]{2,1,0:T(8,128)(2,1)} %shift_ops.1) | copy-start | bytes 786436
  20.8 0.7 %copy-start.5 = (s32[2528]{0:T(1024)S(1)}, s32[2528]{0:T(1024)}, u32[]{:S(2)}) copy-start(s32[2528]{0:T(1024)} %constant.2.clone.wtab) | copy-start | bytes 30340

commit v4 on v3

--- a/solution.py
+++ b/solution.py
@@ -80,18 +80,21 @@
 
 
 def halo_kernel(
-    count, level_bits, fext, gext, fine, parent, fmask, pmask, out_f, out_p, wb,
-    ext_f, ext_p, turned_f, turned_p, sent, got,
+    count, level_bits, fext, gext, fine_in, parent_in, fmask_in, pmask_in, out_f, out_p, wb,
+    ext_f, ext_p, turned_f, turned_p, fine, parent, fmask, pmask, sent, got, fetched,
 ):
+    fetches = [
+        pltpu.make_async_copy(src, dst, fetched.at[k])
+        for k, (src, dst) in enumerate(
+            ((fine_in, fine), (parent_in, parent), (fmask_in, fmask), (pmask_in, pmask))
+        )
+    ]
+    for fetch in fetches:
+        fetch.start()
     me = lax.axis_index("box")
     levels = ((fine, ext_f, fext), (parent, ext_p, gext))
     for _, ext, _ in levels:
         ext[...] = jnp.zeros_like(ext)
-    for block, ext, (sx, sy, sz) in levels:
-        for m in range(sx * sy * sz):
-            at = grid_index(m, (sx, sy, sz))
-            ext[1 + at // (sy * sz), 1 + at // sz % sy, 1 + at % sz] = block[m]
-
     around = []
     for dim in range(3):
         owned = [k for k in range(count.bit_length() - 1) if 2 - (level_bits + k) % 3 == dim]
@@ -113,6 +116,13 @@
                 pl.semaphore_signal(
                     barrier, inc=1, device_id=(dst,), device_id_type=pl.DeviceIdType.MESH
                 )
+    for fetch in fetches:
+        fetch.wait()
+    for block, ext, (sx, sy, sz) in levels:
+        for m in range(sx * sy * sz):
+            at = grid_index(m, (sx, sy, sz))
+            ext[1 + at // (sy * sz), 1 + at // sz % sy, 1 + at % sz] = block[m]
+
     peers = sum(inside.astype(jnp.int32) for sides in around for inside, _ in sides)
     pl.semaphore_wait(barrier, peers)
 
@@ -187,13 +197,21 @@
         out_shape=[
             jax.ShapeDtypeStruct((w[0] * w[1] * w[2] * 8, width), jnp.float32) for w in wide
         ] + [jax.ShapeDtypeStruct((8, 20, sum(boxes) // 128, 16, width), jnp.int16)],
-        in_specs=[vmem] * 4,
+        in_specs=[pl.BlockSpec(memory_space=pltpu.HBM)] * 4,
         out_specs=[vmem] * 3,
         scratch_shapes=[pltpu.VMEM(w + (8, width), jnp.bfloat16) for w in wide]
         + [pltpu.VMEM((b, 128), jnp.int32) for b in boxes]
-        + [pltpu.SemaphoreType.DMA((3, 2, 2)), pltpu.SemaphoreType.DMA((3, 2, 2))],
+        + [
+            pltpu.VMEM((boxes[0] // 8, 8, width), jnp.bfloat16),
+            pltpu.VMEM((boxes[1] // 8, 8, width), jnp.bfloat16),
+            pltpu.VMEM(fine_mask.shape, jnp.int32),
+            pltpu.VMEM(parent_mask.shape, jnp.int32),
+            pltpu.SemaphoreType.DMA((3, 2, 2)),
+            pltpu.SemaphoreType.DMA((3, 2, 2)),
+            pltpu.SemaphoreType.DMA((4,)),
+        ],
         compiler_params=pltpu.CompilerParams(
-            collective_id=0, has_side_effects=True, vmem_limit_bytes=24 * 1024 * 1024
+            collective_id=0, has_side_effects=True, vmem_limit_bytes=54 * 1024 * 1024
         ),
         name="halo",
     )(
@@ -300,7 +318,7 @@
     )
     wtab = window_table()
     smem = pl.BlockSpec(memory_space=pltpu.SMEM)
-    hbm = pl.BlockSpec(memory_space=pl.ANY)
+    hbm = pl.BlockSpec(memory_space=pltpu.HBM)
     vmem = pl.BlockSpec(memory_space=pltpu.VMEM)
     return pl.pallas_call(
         functools.partial(interact_kernel, fext, gext),
@@ -321,7 +339,7 @@
             pltpu.VMEM((nf, width), jnp.float32),
             pltpu.SemaphoreType.DMA((2,)),
         ],
-        compiler_params=pltpu.CompilerParams(vmem_limit_bytes=44 * 1024 * 1024),
+        compiler_params=pltpu.CompilerParams(vmem_limit_bytes=54 * 1024 * 1024),
         cost_estimate=pl.CostEstimate(
             flops=2 * 8 * rows * 189 * width * width,
             bytes_accessed=kernels.size * 2,

time: 49.2 us -> 49.5 us (level)
  Pallas kernels: 42.7 us -> 48.2 us
  local copies, waits for them, and re-layouts: 4.95 us -> 0 us
    unnamed x12 -> x0, local copies, waits for them, and re-layouts: 4.95 us -> none
    pallas_call x1, Pallas kernels: 15.9 us -> 18.9 us  [exchange(): pl.pallas_call(functools.partial(halo_kernel, count, fbits + 3, fext, gex...]
    pallas_call x1, Pallas kernels: 26.9 us -> 29.4 us  [on_device(): pl.pallas_call(functools.partial(interact_kernel, fext, gext), out_shape=...]
where the time goes in v4:
time: 49.5 us; the launch traced here: 49 us
  Pallas kernels  48.2 us (97%)
  between operations  0.8 us (2%)
    pallas_call x1, Pallas kernels, on_device(): pl.pallas_call(functools.partial(interact_kernel, fext, gext), out_shape=...  29.4 us
    pallas_call x1, Pallas kernels, exchange(): pl.pallas_call(functools.partial(halo_kernel, count, fbits + 3, fext, gex...  18.9 us

profile of v4, /device:TPU:3, one launch (start us, length us, event | category | flops | bytes accessed | tf_op | source)
XLA Modules:
  0.0 49.0 jit_solution(3271499084487892254)
XLA Ops:
  0.6 18.9 %halo.1 = (f32[2880,128]{1,0:T(8,128)}, f32[768,128]{1,0:T(8,128)}, s16[8,20,9,16,128]{4,3,2,1,0:T(8,128)(2,1)}) custom-call(bf16[128,8,128]{2,1,0:T(8,128)(2,1)} %bitcast.2, bf16[16,8,128]{2,1,0:T(8,128)(2,1)} %bitcast.3, s32[20,1024]{1,0:T(8,128)} %fmask_in.1, s32[20,128]{1,0:T(8,128)} %pmask_in.1), custom_call_target="tpu_custom_call" | custom-call | tf_op jit(solution)/shard_map/halo/pallas_call | solution.py:195
  19.5 29.4 %interact.1 = (bf16[1024,128]{1,0:T(8,128)(2,1)}, bf16[128,128]{1,0:T(8,128)(2,1)}) custom-call(s32[2528]{0:T(1024)} %constant.2.clone.wtab, f32[2880,128]{1,0:T(8,128)} %get-tuple-element.5.ext_f, f32[768,128]{1,0:T(8,128)} %get-tuple-element.6.ext_p, s16[8,20,9,16,128]{4,3,2,1,0:T(8,128)(2,1)} %get-tuple-element.7.wb, bf16[8,128,128]{2,1,0:T(8,128)(2,1)} %shift_ops.1, ...), custom_call_target="tpu_custom_call" | custom-call | flops 7134511104 | bytes 10354688 | tf_op jit(solution)/shard_map/interact/pallas_call | solution.py:323
